TPU v7x, 32 devices: a whole 2x2x4 slice. The times are simulated.
32 devices in a mesh: dp: 16 (over z, y, x), hidden: 2 (over core).
Axes of the slice: x: 2, y: 2, z: 4, core: 2. Of those that a mesh axis runs over, the one named last changes fastest.
Arguments:
- tokens: float32 [50176, 320], P(('dp', 'hidden')), may hold values from -6 to 6
- block_kind: int32 [256], replicated, may hold values from 0 to 1
- first_gain: float32 [320], replicated, may hold values from 0.25 to 1.75
- first_bias: float32 [320], replicated, may hold values from -1.5 to 1.5
- query_weight: float32 [320, 320], replicated, may hold values from -0.3125 to 0.3125
- query_bias: float32 [320], replicated, may hold values from -1.5 to 1.5
- reduce_weight: float32 [1280, 320], replicated, may hold values from -0.15625 to 0.15625
- reduce_bias: float32 [320], replicated, may hold values from -1.5 to 1.5
- reduce_gain: float32 [320], replicated, may hold values from 0.25 to 1.75
- reduce_shift: float32 [320], replicated, may hold values from -1.5 to 1.5
- keyval_weight: float32 [320, 640], replicated, may hold values from -0.3125 to 0.3125
- value_bias: float32 [320], replicated, may hold values from -1.5 to 1.5
- output_weight: float32 [320, 320], replicated, may hold values from -0.625 to 0.625
- output_bias: float32 [320], replicated, may hold values from -1.5 to 1.5
- second_gain: float32 [320], replicated, may hold values from 0.25 to 1.75
- second_shift: float32 [320], replicated, may hold values from -1.5 to 1.5
- expand_weight: float32 [320, 1280], P(None, 'hidden'), may hold values from -0.3125 to 0.3125
- expand_bias: float32 [1280], P('hidden'), may hold values from -1.5 to 1.5
- depth_weight: float32 [9, 1280], P(None, 'hidden'), may hold values from -2 to 2
- depth_bias: float32 [1280], P('hidden'), may hold values from -1.5 to 1.5
- shrink_weight: float32 [1280, 320], P('hidden'), may hold values from -0.25 to 0.25
- shrink_bias: float32 [320], replicated, may hold values from -1.5 to 1.5
- cotangent: float32 [50176, 320], P(('dp', 'hidden')), may hold values from -6 to 6
Outputs:
- result: float32 [50176, 320], P(('dp', 'hidden'))
- tokens_grad: float32 [50176, 320], P(('dp', 'hidden'))
- grad_first_gain: float32 [320], replicated
- grad_first_bias: float32 [320], replicated
- grad_query_weight: float32 [320, 320], replicated
- grad_query_bias: float32 [320], replicated
- grad_reduce_weight: float32 [1280, 320], replicated
- grad_reduce_bias: float32 [320], replicated
- grad_reduce_gain: float32 [320], replicated
- grad_reduce_shift: float32 [320], replicated
- grad_keyval_weight: float32 [320, 640], replicated
- grad_value_bias: float32 [320], replicated
- grad_output_weight: float32 [320, 320], replicated
- grad_output_bias: float32 [320], replicated
- grad_second_gain: float32 [320], replicated
- grad_second_shift: float32 [320], replicated
- grad_expand_weight: float32 [320, 1280], P(None, 'hidden')
- grad_expand_bias: float32 [1280], P('hidden')
- grad_depth_weight: float32 [9, 1280], P(None, 'hidden')
- grad_depth_bias: float32 [1280], P('hidden')
- grad_shrink_weight: float32 [1280, 320], P('hidden')
- grad_shrink_bias: float32 [320], replicated
Inputs may be any that keep to these rules, and one draw needn't show every extreme that they name: `block_kind`: 0: one 224 crop as a 14 x 14 grid; 1: 5 96 crops of 6 x 6 rows each, then empty rows.
All inputs are finite; a program needn't handle non-finite values.
Results may differ from a plain program's by a relative error of at most 0.0003.
Values sent between devices are 32-bit elements; how exact they have to be, the bound alone decides.
A program may use at most 384 MiB of HBM per device.

v0:
```python
from functools import partial

import jax
import jax.numpy as jnp
import numpy as np
from jax import lax
from jax.experimental import pallas as pl
from jax.experimental.pallas import tpu as pltpu
from jax.sharding import PartitionSpec as P

HEADS = 5
HEAD = 64
BLOCK = 196
GRID = 14
SMALL = 6
SMALL_IMGS = 5
KVB = 49
D = 320
FF = 1280
KPAD = 56
WIN = 208
ODD = 184
CHUNK = 256
CHUNKS = FF // CHUNK
SLAB = 224
PAD = 16
MIB = 1024 * 1024

f32 = jnp.float32
bf16 = jnp.bfloat16
MESH = pl.DeviceIdType.MESH


def gather_table():
    out = np.zeros((2, 2, 4 * KPAD, WIN), np.float32)
    for kind in range(2):
        for parity in range(2):
            off = 12 * parity
            for a in range(2):
                for b in range(2):
                    for key in range(KVB):
                        if kind == 0:
                            i, j = divmod(key, GRID // 2)
                            spot = (2 * i + a) * GRID + 2 * j + b
                        else:
                            if key >= 45:
                                continue
                            image, rest = divmod(key, 9)
                            i, j = divmod(rest, 3)
                            spot = image * 36 + (2 * i + a) * SMALL + 2 * j + b
                        out[kind, parity, (2 * a + b) * KPAD + key, off + spot] = 1.0
    return out.reshape(4, 4 * KPAD, WIN)


def score_table():
    out = np.full((2, 2, WIN, 256), -1e30, np.float32)
    for kind in range(2):
        for parity in range(2):
            off = 12 * parity
            for row in range(WIN):
                local = row - off
                for key in range(KVB):
                    if kind == 0 or local < 0 or local >= BLOCK:
                        good = True
                    else:
                        good = key < 45 and key // 9 == min(local // 36, 4)
                    if good:
                        for head in range(HEADS):
                            out[kind, parity, row, head * KVB + key] = 0.0
    return out.reshape(4, WIN, 256)


def row_table():
    out = np.zeros((2, 2, WIN, 128), np.float32)
    for parity in range(2):
        off = 12 * parity
        for row in range(BLOCK):
            i, j = divmod(row, GRID)
            out[0, parity, off + row, :7] = (1, j > 0, j < 13, i > 0, 0, i < 13, 0)
            if row < 180:
                i, j = divmod(row % 36, SMALL)
                out[1, parity, off + row, :7] = (1, j > 0, j < 5, 0, i > 0, 0, i < 5)
    return out.reshape(4, WIN, 128)


def split(x):
    high = x.astype(bf16)
    return high, (x - high.astype(f32)).astype(bf16)


def pack_left(x):
    high = x.astype(bf16).astype(f32)
    low = x - high
    tail = jnp.concatenate([high[:, 256:], low[:, 256:]], 1).astype(bf16)
    high, low = high[:, :256].astype(bf16), low[:, :256].astype(bf16)
    return jnp.concatenate([high, low, high, tail, tail], 1)


def pack_short(x):
    high = x.astype(bf16).astype(f32)
    low = x - high
    tail = jnp.concatenate([high[:, 256:], low[:, 256:]], 1).astype(bf16)
    return jnp.concatenate([high[:, :256].astype(bf16), low[:, :256].astype(bf16), tail], 1)


def pack_lane(w):
    high = w.astype(bf16).astype(f32)
    low = w - high
    tail_high = jnp.concatenate([high[:, 256:], high[:, 256:]], 1).astype(bf16)
    tail_low = jnp.concatenate([low[:, 256:], low[:, 256:]], 1).astype(bf16)
    high, low = high[:, :256].astype(bf16), low[:, :256].astype(bf16)
    return jnp.concatenate([high, high, low, tail_high, tail_low], 1)


def pack_down(w):
    high, low = split(w)
    return jnp.concatenate(
        [high[:256], high[:256], low[:256], high[256:], high[256:], low[256:], low[256:]], 0
    )


def triple_left(x):
    high, low = split(x)
    return jnp.concatenate([high, low, high], 1)


def triple_down(w):
    high, low = split(w)
    return jnp.concatenate([high, high, low], 0)


def triple_lane(w):
    high, low = split(w)
    return jnp.concatenate([high, high, low], 1)


def mm(a, b):
    return jnp.dot(a, b, preferred_element_type=f32)


def mm_lane(a, b):
    return lax.dot_general(a, b, (((1,), (1,)), ((), ())), preferred_element_type=f32)


def mm_rows(a, b):
    left_high, left_low = split(a.T)
    high, low = split(b)
    return mm(left_high, high) + mm(left_low, high) + mm(left_high, low)


def norm_rows(x):
    center = jnp.sum(x, -1, keepdims=True) * (1.0 / D)
    centered = x - center
    spread = jnp.sum(centered * centered, -1, keepdims=True) * (1.0 / D)
    scale = lax.rsqrt(spread + 1e-06)
    return centered * scale, scale


def norm_back(h, n, scale):
    mean_h = jnp.sum(h, -1, keepdims=True) * (1.0 / D)
    mean_hn = jnp.sum(h * n, -1, keepdims=True) * (1.0 / D)
    return scale * (h - mean_h - n * mean_hn)


def fold(x):
    return jnp.sum(x.reshape(x.shape[0] // 8, 8, x.shape[1]), 0)


def window(block):
    return pl.multiple_of((block // 2) * (2 * BLOCK) + (block % 2) * ODD, 8)


def slab(w):
    return pl.ds(pl.multiple_of(w * SLAB, SLAB), SLAB)


def place_window(ref, block, value):
    start = window(block)

    @pl.when(block % 2 == 0)
    def _():
        ref[pl.ds(start, WIN), :] = value

    @pl.when(block % 2 == 1)
    def _():
        edge = ref[pl.ds(start + 8, 8), :]
        rows = lax.broadcasted_iota(jnp.int32, edge.shape, 0)
        ref[pl.ds(start + 8, 8), :] = jnp.where(rows < 4, edge, value[8:16])
        ref[pl.ds(start + 16, WIN - 16), :] = value[16:]


def head_block(rows_ref, block, out_ref):
    start = pl.multiple_of(block * KPAD, 8)
    for head in range(HEADS):
        tile = head // 2
        if tile < 2:
            value = rows_ref[pl.ds(start, KPAD), tile * 128 : tile * 128 + 128]
            lane = lax.broadcasted_iota(jnp.int32, value.shape, 1)
            value = jnp.where((lane >= 64) == (head % 2 == 1), value, 0.0)
        else:
            half = rows_ref[pl.ds(start, KPAD), 256:320]
            value = jnp.concatenate([half, half], 1)
        out_ref[tile, head * KVB : head * KVB + KVB, :] = value[:KVB]


def head_rows(ref):
    return jnp.concatenate([ref[0], ref[1], ref[2][:, :64]], 1)


def head_unblock(ref, value):
    ref[0] = value[:, :128]
    ref[1] = value[:, 128:256]
    ref[2] = jnp.concatenate([value[:, 256:], value[:, 256:]], 1)
    lane = lax.broadcasted_iota(jnp.int32, (KPAD, 128), 1)
    row = lax.broadcasted_iota(jnp.int32, (KPAD, 128), 0)
    tiles = []
    for tile in range(3):
        first = ref[tile, 2 * tile * KVB : 2 * tile * KVB + KPAD, :]
        if tile < 2:
            second = ref[tile, (2 * tile + 1) * KVB : (2 * tile + 1) * KVB + KPAD, :]
            first = jnp.where(lane < 64, first, second)
        tiles.append(jnp.where(row < KVB, first, 0.0))
    return jnp.concatenate([tiles[0], tiles[1], tiles[2][:, :64]], 1)


def head_lane(ref):
    parts = []
    for tile in range(3):
        high = ref[tile].astype(bf16)
        parts.append((high, (ref[tile] - high.astype(f32)).astype(bf16)))
    return jnp.concatenate(
        [parts[0][0], parts[1][0], parts[0][0], parts[1][0], parts[0][1], parts[1][1], parts[2][0], parts[2][1]], 1
    )


def head_of_lane(shape):
    lane = lax.broadcasted_iota(jnp.int32, shape, 1)
    return [lane < (head + 1) * KVB for head in range(HEADS - 1)]


def by_head(below, values):
    out = values[HEADS - 1]
    for head in range(HEADS - 2, -1, -1):
        out = jnp.where(below[head], values[head], out)
    return out


def per_head(below, x, empty, reduce):
    out = []
    for head in range(HEADS):
        here = x
        if head < HEADS - 1:
            here = jnp.where(below[head], here, empty)
        if head > 0:
            here = jnp.where(below[head - 1], empty, here)
        out.append(reduce(here, axis=1, keepdims=True))
    return by_head(below, [jnp.broadcast_to(v, x.shape) for v in out])


def line(ref):
    return ref[...].reshape(1, -1)


def own_first(blocks):
    return (lax.axis_index("dp") * lax.axis_size("hidden") + lax.axis_index("hidden")) * blocks


def attention_kernel(
    kinds,
    tokens_t,
    table,
    scores_mask,
    row_marks,
    first_gain,
    first_bias,
    query_bias,
    reduce_bias,
    reduce_gain,
    reduce_shift,
    value_bias,
    output_bias,
    wq,
    wr,
    wkv,
    wo,
    after,
    marks,
    first_n,
    query,
    attended,
    probs,
    keys,
    values,
    red_n,
    patches,
    wq_s,
    wo_s,
    wk_s,
    wv_s,
    wr_s,
    tokens,
    normed,
    kb,
    vb,
):
    blocks = probs.shape[0]
    slabs = tokens.shape[0] // SLAB
    first = own_first(blocks)
    g1, b1, bq, br = line(first_gain), line(first_bias), line(query_bias), line(reduce_bias)
    gr, sr, bv, bo = line(reduce_gain), line(reduce_shift), line(value_bias), line(output_bias)
    wq_s[...] = pack_down(wq[...])
    wo_s[...] = pack_down(wo[...])
    wk_s[...] = pack_down(wkv[:, :D])
    wv_s[...] = pack_down(wkv[:, D:])
    for sub in range(4):
        wr_s[sub] = pack_lane(wr[:, sub * D : sub * D + D])
    kb[...] = jnp.zeros_like(kb)
    vb[...] = jnp.zeros_like(vb)
    tokens[...] = tokens_t[...].T

    @pl.loop(0, slabs)
    def _(w):
        n, scale = norm_rows(tokens[slab(w), :])
        first_n[slab(w), :] = jnp.concatenate([n, jnp.broadcast_to(scale, (SLAB, 64))], 1)
        n = n * g1 + b1
        normed[slab(w), :] = n
        query[slab(w), :] = mm(pack_left(n), wq_s[...]) + bq

    @pl.loop(0, blocks)
    def _(b):
        which = kinds[first + b] * 2 + b % 2
        place_window(marks, b, row_marks[which])
        part = normed[pl.ds(window(b), WIN), :]
        high, low = split(part)
        pick = table[which]
        got = mm(pick, high) + mm(pick, low)
        rows = pl.ds(pl.multiple_of(b * KPAD, 8), KPAD)
        for sub in range(4):
            patches[sub, rows, :] = got[sub * KPAD : sub * KPAD + KPAD]

    @pl.loop(0, blocks * KPAD // SLAB)
    def _(w):
        acc = br + mm_lane(pack_left(patches[0, slab(w), :]), wr_s[0])
        for sub in range(1, 4):
            acc = acc + mm_lane(pack_left(patches[sub, slab(w), :]), wr_s[sub])
        n, scale = norm_rows(acc)
        red_n[slab(w), :] = jnp.concatenate([n, jnp.broadcast_to(scale, (SLAB, 64))], 1)
        packed = pack_left(n * gr + sr)
        keys[slab(w), :] = mm(packed, wk_s[...])
        values[slab(w), :] = mm(packed, wv_s[...]) + bv

    @pl.loop(0, blocks)
    def _(b):
        which = kinds[first + b] * 2 + b % 2
        head_block(keys, b, kb)
        head_block(values, b, vb)
        q = query[pl.ds(window(b), WIN), :]
        s = mm_lane(pack_left(q), head_lane(kb)) * (HEAD**-0.5) + scores_mask[which]
        below = head_of_lane(s.shape)
        e = jnp.exp(s - per_head(below, s, -3e38, jnp.max))
        p = e / per_head(below, e, 0.0, jnp.sum)
        probs[b] = p
        out = mm(triple_left(p), triple_down(head_rows(vb)))
        place_window(attended, b, out)

    @pl.loop(0, slabs)
    def _(w):
        branch = mm(pack_left(attended[slab(w), :]), wo_s[...]) + bo
        after[slab(w), :] = tokens[slab(w), :] + marks[slab(w), 0:1] * branch


def attention_forward(kinds, tokens_t, vecs, wq, wr, wkv, wo):
    rows = tokens_t.shape[1]
    blocks = rows // BLOCK
    krows = blocks * KPAD
    vm = pl.BlockSpec(memory_space=pltpu.VMEM)

    def shape(*dims):
        return jax.ShapeDtypeStruct(dims, f32)

    return pl.pallas_call(
        attention_kernel,
        out_shape=(
            shape(rows, D),
            shape(rows, 128),
            shape(rows, D + 64),
            shape(rows, D),
            shape(rows, D),
            shape(blocks, WIN, 256),
            shape(krows, D),
            shape(krows, D),
            shape(krows, D + 64),
            shape(4, krows, D),
        ),
        in_specs=[pl.BlockSpec(memory_space=pltpu.SMEM)] + [vm] * 16,
        out_specs=(vm,) * 10,
        scratch_shapes=[
            pltpu.VMEM((1024, D), bf16),
            pltpu.VMEM((1024, D), bf16),
            pltpu.VMEM((1024, D), bf16),
            pltpu.VMEM((1024, D), bf16),
            pltpu.VMEM((4, D, 1024), bf16),
            pltpu.VMEM((rows, D), f32),
            pltpu.VMEM((rows, D), f32),
            pltpu.VMEM((3, 256, 128), f32),
            pltpu.VMEM((3, 256, 128), f32),
        ],
        compiler_params=pltpu.CompilerParams(vmem_limit_bytes=60 * MIB),
        name="attention",
    )(
        kinds,
        tokens_t,
        jnp.asarray(gather_table(), bf16),
        jnp.asarray(score_table()),
        jnp.asarray(row_table()),
        *vecs,
        wq,
        wr,
        wkv,
        wo,
    )


ERF_P = 0.3275911
ERF = (0.254829592, -0.284496736, 1.421413741, -1.453152027, 1.061405429)


def gelu_pair(x):
    size = jnp.abs(x)
    d = 1.0 + (ERF_P * 0.7071067811865476) * size
    t = pl.reciprocal(d, approx=True)
    t = t * (2.0 - d * t)
    e = jnp.exp(-0.5 * (x * x))
    poly = t * (ERF[0] + t * (ERF[1] + t * (ERF[2] + t * (ERF[3] + t * ERF[4]))))
    tail = 0.5 * (poly * e)
    phi = jnp.where(x < 0.0, tail, 1.0 - tail)
    return x * phi, phi + x * (0.3989422804014327 * e)


def has_left(r):
    return r % GRID > 0, r < 180 and r % SMALL > 0


def has_right(r):
    return r % GRID < GRID - 1, r < 180 and r % SMALL < SMALL - 1


def has_up(r):
    return r >= GRID, r < 180 and r % 36 >= SMALL


def has_down(r):
    return r < BLOCK - GRID, r < 180 and r % 36 < 30


def total_of(values):
    values = [v for v in values if v is not None]
    out = values[0]
    for v in values[1:]:
        out = out + v
    return out


def forward_kernel(
    kinds,
    after,
    cot_t,
    second_gain,
    second_shift,
    shrink_bias,
    own_we,
    own_ws,
    own_taps,
    result_t,
    g_after,
    pack,
    sums,
    we_s,
    we_l,
    ws_s,
    ws_l,
    result,
    g_second,
    by_block,
    by_place,
    taps,
    second,
    branch,
    second_t,
    branch_t,
    xs0,
    xs1,
    nx1,
    ga0,
    ga1,
    ng1,
    y0,
    yu,
    yd,
    act,
    gx,
    held_act,
    held_gx,
    sem,
):
    rows = after.shape[0]
    part = rows // 2
    per = FF // 128 // own_we.shape[0]
    g2, s2, bs = line(second_gain), line(second_shift), line(shrink_bias)
    first = own_first(8)
    block = lax.broadcasted_iota(jnp.int32, (8, 128), 0)
    kind = jnp.zeros((8, 128), jnp.int32)
    for i in range(8):
        kind = jnp.where(block == i, kinds[first + i], kind)
    zero_kind = kind == 0
    k0 = jnp.where(zero_kind, 1.0, 0.0)
    k1 = 1.0 - k0

    loads = []
    for tile in range(FF // 128):
        lanes = pl.ds((tile % per) * 128, 128)
        for i, (source, low, size) in enumerate(((own_we, 0, D), (own_ws, D, D), (own_taps, 2 * D, 16))):
            loads.append(
                pltpu.make_async_copy(
                    source.at[tile // per, :, lanes], pack.at[tile, pl.ds(low, size)], sem.at[3 * tile + i]
                )
            )
    for load in loads:
        load.start()

    held_act[...] = jnp.zeros_like(held_act)
    held_gx[...] = jnp.zeros_like(held_gx)
    sums[...] = jnp.zeros_like(sums)

    def tiles_of(x):
        return x[:, :128], x[:, 128:256], jnp.concatenate([x[:, 256:], x[:, 256:]], 1)

    def to_places(out):
        for t in range(3):
            for i in range(8):
                by_place[t, pl.ds(i, BLOCK, stride=8), :] = by_block[t, i * BLOCK : (i + 1) * BLOCK, :]

        @pl.loop(0, rows // SLAB)
        def _(w):
            out[slab(w), :] = joined(by_place, slab(w))

    def to_blocks(source):
        @pl.loop(0, rows // SLAB)
        def _(w):
            for t, value in enumerate(tiles_of(source[slab(w), :])):
                by_place[t, slab(w), :] = value

        for t in range(3):
            for i in range(8):
                by_block[t, i * BLOCK : (i + 1) * BLOCK, :] = by_place[t, pl.ds(i, BLOCK, stride=8), :]

    def joined(ref, at):
        return jnp.concatenate([ref[0, at, :], ref[1, at, :], ref[2, at, :][:, :64]], 1)

    for t in range(3):
        low, high = 128 * t, min(128 * t + 128, D)
        value = cot_t[low:high, :].T
        by_block[t] = value if high - low == 128 else jnp.concatenate([value, value], 1)
    to_places(result)

    @pl.loop(0, rows // SLAB)
    def _(w):
        for t, value in enumerate(tiles_of(after[slab(w), :])):
            by_block[t, slab(w), :] = value

    to_places(g_second)

    g_after[...] = result[...]
    dead = 180 * 8
    result[dead:, :] = (result[dead:, :].reshape(BLOCK - 180, 8, D) * k0[:, :1]).reshape(rows - dead, D)

    @pl.loop(0, rows // SLAB)
    def _(w):
        a = g_second[slab(w), :]
        for t, value in enumerate(tiles_of(a)):
            by_block[t, slab(w), :] = value
        n, _ = norm_rows(a)
        value = n * g2 + s2
        g_second[slab(w), :] = value
        second[slab(w), :] = pack_short(value)
        grad = result[slab(w), :]
        sums[2] += fold(grad)
        branch[slab(w), :] = pack_short(grad)

    for source, turned in ((g_second, second_t), (result, branch_t)):
        high, low = split(source[...].T)
        turned[...] = jnp.concatenate([high, low, high], 1)
    result[...] = jnp.zeros_like(result)
    g_second[...] = jnp.zeros_like(g_second)

    for load in loads:
        load.wait()
    for c in range(CHUNKS):
        for which, (down, lane) in enumerate(((we_s, we_l), (ws_s, ws_l))):
            value = jnp.concatenate([pack[2 * c + t, which * D : which * D + D, :] for t in range(2)], 1)
            high, low = split(value)
            down[c] = jnp.concatenate([high, low], 0)
            lane[c] = jnp.concatenate([high, low], 1)
        for t in range(2):
            for k in range(11):
                taps[c, t, k] = jnp.broadcast_to(pack[2 * c + t, 2 * D + k : 2 * D + k + 1, :], (8, 128))

    def own(h):
        return slice(h * part, (h + 1) * part)

    def left(ref, h):
        x = ref[own(h), :]
        return jnp.concatenate([x[:, :512], x[:, :256], x[:, 512:], x[:, 512:]], 1)

    def deep(ref, c):
        x = ref[c]
        return jnp.concatenate(
            [x[:256], x[:256], x[D : D + 256], x[256:D], x[256:D], x[D + 256 :], x[D + 256 :]], 0
        )

    def expand_task(c, h, outs):
        e = mm(left(second, h), deep(we_s, c))
        for t in range(2):
            outs[t][own(h), :] = e[:, 128 * t : 128 * t + 128] + taps[c, t, 9][0:1]

    def active_grad_task(c, h, outs):
        g = mm(left(branch, h), deep(ws_s, c))
        for t in range(2):
            outs[t][own(h), :] = g[:, 128 * t : 128 * t + 128]

    def out_task(c, h, source, lane, out):
        x = source[own(h), :]
        weight = lane[c]
        out[own(h), :] += mm_lane(
            jnp.concatenate([x, x[:, :256]], 1), jnp.concatenate([weight[:, :256], weight], 1)
        )

    def weight_task(c, source, turned, row):
        high, low = source[:, :256], source[:, 256:]
        value = mm(turned[...], jnp.concatenate([high, high, low], 0))
        for t in range(2):
            pack[2 * c + t, row : row + D, :] = value[:, 128 * t : 128 * t + 128]

    def early_tasks(c, x_outs, g_outs):
        return [partial(expand_task, c, h, x_outs) for h in range(2)] + [
            partial(active_grad_task, c, h, g_outs) for h in range(2)
        ]

    def late_tasks(c):
        return [
            partial(out_task, c, 0, held_act, ws_l, result),
            partial(out_task, c, 0, held_gx, we_l, g_second),
            partial(out_task, c, 1, held_act, ws_l, result),
            partial(out_task, c, 1, held_gx, we_l, g_second),
        ]

    def weight_tasks(c):
        return [
            partial(weight_task, c, held_act, branch_t, D),
            partial(weight_task, c, held_gx, second_t, 0),
        ]

    def at(r):
        return slice(8 * r, 8 * r + 8)

    def gated(value, ok):
        if ok[0] and ok[1]:
            return value
        if ok[0]:
            return value * k0
        return value * k1 if ok[1] else None

    def picked(ref, r, ok, sign):
        if ok[0] and ok[1]:
            return jnp.where(zero_kind, ref[at(r + sign * GRID), :], ref[at(r + sign * SMALL), :])
        if ok[0]:
            return ref[at(r + sign * GRID), :] * k0
        return ref[at(r + sign * SMALL), :] * k1 if ok[1] else None

    def put_split(ref, t, r, pair):
        high, low = split(jnp.concatenate(pair, 0))
        here = slice(8 * r, 8 * r + 16)
        ref[here, 128 * t : 128 * t + 128] = high
        ref[here, 256 + 128 * t : 384 + 128 * t] = low

    def item(c, t, x, g, tasks):
        tap = [taps[c, t, k] for k in range(11)]
        totals = [jnp.zeros((8, 128), f32)] * 11

        def columns(r, near):
            return [
                gated(near(r - 1), has_left(r)) if r > 0 else None,
                near(r),
                gated(near(r + 1), has_right(r)) if r + 1 < BLOCK else None,
            ]

        def mix(values, ks, more=()):
            return total_of([None if v is None else v * tap[k] for v, k in zip(values, ks)] + list(more))

        def loader():
            kept = {}

            def near(r):
                if r not in kept:
                    kept[r] = x[at(r), :]
                return kept[r]

            return near

        ahead, behind = loader(), loader()
        moved_back = {}
        every = {}
        count = (BLOCK + 30) // 2
        slots = {round((i + 0.5) * count / len(tasks)): task for i, task in enumerate(tasks)}
        for step in range(count):
            for r in (2 * step, 2 * step + 1):
                if r < BLOCK:
                    cols = columns(r, ahead)
                    yu[at(r), :] = mix(cols, (0, 1, 2))
                    y0[at(r), :] = mix(cols, (3, 4, 5), (tap[10],))
                    yd[at(r), :] = mix(cols, (6, 7, 8))
            r = 2 * step - 14
            if 0 <= r < BLOCK:
                conv = [
                    total_of([y0[at(s), :], picked(yu, s, has_up(s), -1), picked(yd, s, has_down(s), 1)])
                    for s in (r, r + 1)
                ]
                active, slope = gelu_pair(jnp.concatenate(conv, 0))
                put_split(act, t, r, [active[:8], active[8:]])
                here = slice(8 * r, 8 * r + 16)
                g[here, :] = g[here, :] * slope
            for r in (2 * step - 28, 2 * step - 27):
                if 0 <= r < BLOCK:
                    same = g[at(r), :]
                    moved = [picked(g, r, has_down(r), 1), same, picked(g, r, has_up(r), -1)]
                    cols = columns(r, behind)
                    totals[10] = totals[10] + same
                    for p in range(3):
                        for q in range(3):
                            if moved[p] is not None and cols[q] is not None:
                                totals[3 * p + q] = totals[3 * p + q] + moved[p] * cols[q]
                    moved_back[r] = [mix(moved, ks) for ks in ((0, 3, 6), (1, 4, 7), (2, 5, 8))]
            r = 2 * step - 30
            if 0 <= r < BLOCK:
                pair = []
                for s in (r, r + 1):
                    value = total_of(
                        [
                            moved_back[s][1],
                            gated(moved_back[s - 1][2], has_left(s)) if s > 0 else None,
                            gated(moved_back[s + 1][0], has_right(s)) if s + 1 < BLOCK else None,
                        ]
                    )
                    totals[9] = totals[9] + value
                    pair.append(value)
                put_split(gx, t, r, pair)
            if step in slots:
                slots[step]()
        for k in range(11):
            pack[2 * c + t, 2 * D + k : 2 * D + k + 1, :] = jnp.sum(totals[k], 0, keepdims=True)

    for task in early_tasks(0, (xs0, xs1), (ga0, ga1)):
        task()

    @pl.loop(0, CHUNKS)
    def _(c):
        before = jnp.maximum(c - 1, 0)
        item(c, 0, xs0, ga0, late_tasks(before) + weight_tasks(before)[:1])
        later = jnp.minimum(c + 1, CHUNKS - 1)
        item(c, 1, xs1, ga1, early_tasks(later, (xs0, nx1), (ga0, ng1)) + weight_tasks(before)[1:])
        xs1[...] = nx1[...]
        ga1[...] = ng1[...]
        held_act[...] = act[...]
        held_gx[...] = gx[...]

    for task in late_tasks(CHUNKS - 1) + weight_tasks(CHUNKS - 1):
        task()
    for c in range(CHUNKS):
        for t in range(2):
            pack[2 * c + t, 2 * D + 11 : 2 * D + 16, :] = jnp.zeros((5, 128), f32)

    result[dead:, :] = ((result[dead:, :] + bs).reshape(BLOCK - 180, 8, D) * k0[:, :1]).reshape(rows - dead, D) - bs

    @pl.loop(0, rows // SLAB)
    def _(w):
        a = joined(by_block, slab(w))
        result[slab(w), :] = a + (result[slab(w), :] + bs)
        n, scale = norm_rows(a)
        g = g_second[slab(w), :]
        sums[0] += fold(g * n)
        sums[1] += fold(g)
        g_second[slab(w), :] = g_after[slab(w), :] + norm_back(g * g2, n, scale)

    to_blocks(result)
    for t in range(3):
        low, high = 128 * t, min(128 * t + 128, D)
        result_t[low:high, :] = by_block[t].T[: high - low]
    to_blocks(g_second)

    @pl.loop(0, rows // SLAB)
    def _(w):
        g_after[slab(w), :] = joined(by_block, slab(w))


def feed_forward(kinds, after, cot_t, vecs, weights):
    rows = after.shape[0]
    vm = pl.BlockSpec(memory_space=pltpu.VMEM)
    tile = pltpu.VMEM((rows, 128), f32)
    half = pltpu.VMEM((rows, 2 * CHUNK), bf16)
    return pl.pallas_call(
        forward_kernel,
        out_shape=(
            jax.ShapeDtypeStruct((D, rows), f32),
            jax.ShapeDtypeStruct((rows, D), f32),
            jax.ShapeDtypeStruct((2 * CHUNKS, 2 * D + 16, 128), f32),
            jax.ShapeDtypeStruct((3, 8, D), f32),
        ),
        in_specs=[pl.BlockSpec(memory_space=pltpu.SMEM)] + [vm] * 5 + [pl.BlockSpec(memory_space=pl.ANY)] * 3,
        out_specs=(vm,) * 4,
        scratch_shapes=[
            pltpu.VMEM((CHUNKS, 2 * D, CHUNK), bf16),
            pltpu.VMEM((CHUNKS, D, 2 * CHUNK), bf16),
            pltpu.VMEM((CHUNKS, 2 * D, CHUNK), bf16),
            pltpu.VMEM((CHUNKS, D, 2 * CHUNK), bf16),
            pltpu.VMEM((rows, D), f32),
            pltpu.VMEM((rows, D), f32),
            pltpu.VMEM((3, rows, 128), f32),
            pltpu.VMEM((3, rows, 128), f32),
            pltpu.VMEM((CHUNKS, 2, 11, 8, 128), f32),
            pltpu.VMEM((rows, 640), bf16),
            pltpu.VMEM((rows, 640), bf16),
            pltpu.VMEM((D, 3 * rows), bf16),
            pltpu.VMEM((D, 3 * rows), bf16),
        ]
        + [tile] * 9
        + [half] * 4
        + [pltpu.SemaphoreType.DMA((6 * CHUNKS,))],
        compiler_params=pltpu.CompilerParams(vmem_limit_bytes=63 * MIB),
        name="feed_forward",
    )(kinds, after, cot_t, *vecs, *weights)


class Wires:
    def __init__(self, pairs, cores, send, recv):
        self.bits = pairs.bit_length() - 1
        self.cores = cores
        self.me, self.core = lax.axis_index("dp"), lax.axis_index("hidden")
        self.other = cores - 1 - self.core
        self.send, self.recv, self.used = send, recv, 0

    def groups(self):
        rest = list(range(2, self.bits))
        return [(k,) for k in range(min(2, self.bits))] + [tuple(rest[i : i + 2]) for i in range(0, len(rest), 2)]

    def bit(self, k):
        return (self.me // (1 << k)) % 2

    def peer(self, group, j):
        flips = [(1 - 2 * self.bit(k)) * (1 << k) for i, k in enumerate(group) if (j >> i) & 1]
        return (sum(flips, self.me), self.core)

    def place(self, group, j):
        bits = [(1 - self.bit(k) if (j >> i) & 1 else self.bit(k)) * (1 << i) for i, k in enumerate(group)]
        return sum(bits[1:], bits[0])

    def greet(self):
        peers = [self.peer(group, j) for group in self.groups() for j in range(1, 1 << len(group))]
        if self.cores > 1:
            peers.append((self.me, self.other))
        if not peers:
            return
        barrier = pltpu.get_barrier_semaphore()
        for target in peers:
            pl.semaphore_signal(barrier, inc=1, device_id=target, device_id_type=MESH)
        pl.semaphore_wait(barrier, len(peers))

    def copy(self, src, dst, target):
        slot = self.used
        self.used += 1
        return pltpu.make_async_remote_copy(
            src_ref=src,
            dst_ref=dst,
            send_sem=self.send.at[slot],
            recv_sem=self.recv.at[slot],
            device_id=target,
            device_id_type=MESH,
        )

    def local(self, src, dst):
        slot = self.used
        self.used += 1
        return pltpu.make_async_copy(src, dst, self.send.at[slot])

    def sibling(self, src, dst):
        return self.copy(src, dst, (self.me, self.other))


def rows_of(start, size):
    return pl.ds(pl.multiple_of(start, 8), size)


class Chain:
    def __init__(self, wires, acc, near, got, full, base, rows, order, opening, closing):
        self.stages, self.costs = [], []
        whole = pl.ds(base, rows)
        scale = 512 * wires.cores / LINK

        def meet():
            if near is not None:
                acc[whole, :] = acc[whole, :] + near[whole, :]

        start, size, spot = base + 0 * wires.me, rows, base
        pending, action = opening, meet
        self.stages.append(([], None, opening))
        self.costs.append(("core", rows * 512 / CORE_LINK))
        held = []
        for group in order:
            many = 1 << len(group)
            size //= many
            keep = start + wires.place(group, 0) * size
            copies, lands = [], []
            for j in range(1, many):
                land = pl.ds(spot, size)
                spot += size
                give = start + wires.place(group, j) * size
                copies.append(wires.copy(acc.at[rows_of(give, size)], got.at[land], wires.peer(group, j)))
                lands.append(land)
            self.stages.append((pending, action, copies))
            self.costs.append((group, scale * size * (1 if many == 2 else many)))

            def add(keep=keep, lands=lands, size=size):
                value = acc[rows_of(keep, size), :]
                for land in lands:
                    value = value + got[land, :]
                acc[rows_of(keep, size), :] = value

            pending, action = copies, add
            held.append((group, start))
            start = keep
        last, last_start, last_size = action, start, size

        def settle():
            last()
            full[rows_of(last_start, last_size), :] = acc[rows_of(last_start, last_size), :]

        action = settle
        for group, before in reversed(held):
            mine = rows_of(start, size)
            many = 1 << len(group)
            copies = [wires.copy(full.at[mine], full.at[mine], wires.peer(group, j)) for j in range(1, many)]
            self.stages.append((pending, action, copies))
            self.costs.append((group, scale * size * (1 if many == 2 else many)))
            pending, action = copies, None
            start, size = before, size * many
        if closing:
            self.stages.append((pending, action, closing))
            self.costs.append(("core", rows * 512 / CORE_LINK))
            pending, action = closing, None
        self.stages.append((pending, action, []))
        self.costs.append((None, 0.0))

    def run(self, stage):
        waits, action, starts = self.stages[stage]
        for c in waits:
            c.wait()
        if action is not None:
            action()
        for c in starts:
            c.start()


class Exchange(Chain):
    def __init__(self, wires, sums, got):
        partners = [((k,), wires.peer((k,), 1)) for k in range(wires.bits)]
        if wires.cores > 1:
            partners.insert(0, ("core", (wires.me, wires.other)))
        self.stages, self.costs = [], []
        pending, action = [], None
        for i, (name, target) in enumerate(partners):
            c = wires.copy(sums.at[i], got.at[i], target)
            self.stages.append((pending, action, [c]))
            self.costs.append((name, 0.5))

            def add(i=i):
                sums[i + 1] = sums[i] + got[i]

            pending, action = [c], add
        self.stages.append((pending, action, []))
        self.costs.append((None, 0.0))
        self.last = len(partners)


LINK = 100e3
CORE_LINK = 400e3
DELAY = 1.5
STEP_WORK = 0.1


class Plan:
    def __init__(self):
        self.now, self.free, self.going = 0.0, {}, []

    def add(self, chains):
        self.going += [[self.now, c, 0] for c in chains]

    def after(self, us):
        self.now += us
        due = []
        while True:
            ready = [g for g in self.going if g[0] <= self.now]
            if not ready:
                return due
            due.append(self.take(min(ready, key=lambda g: g[0])))

    def take(self, entry):
        done, chain, stage = entry
        self.now = max(self.now, done) + STEP_WORK
        link, us = chain.costs[stage]
        self.free[link] = max(self.free.get(link, 0.0), self.now) + us
        if stage + 1 == len(chain.stages):
            self.going.remove(entry)
        else:
            entry[0], entry[2] = self.free[link] + DELAY, stage + 1
        return chain, stage

    def rest(self):
        due = []
        while self.going:
            due.append(self.take(min(self.going, key=lambda g: g[0])))
        return due


def run_steps(steps):
    for chain, stage in steps:
        chain.run(stage)


def axis_orders(groups):
    return groups, groups[1::-1] + groups[2:], groups[2:] + groups[:2]


def cut(total, unit, parts):
    units = total // unit
    marks = sorted({0, units} | {round(units * x) for x in parts})
    return [(a * unit, b * unit) for a, b in zip(marks, marks[1:])]


def round_up(x, unit):
    return -(-x // unit) * unit


def sum_rows(pairs, cores):
    unit = 8 * pairs
    ff = round_up(2 * CHUNKS // cores * (2 * D + 16), unit)
    rest = round_up(20 * (D // cores), unit)
    return ff, rest


def backward_kernel(
    pairs,
    cores,
    kinds,
    first_n,
    g_after,
    marks,
    table,
    first_gain,
    first_bias,
    reduce_gain,
    reduce_shift,
    wq,
    wr,
    wkv,
    wo,
    query,
    attended,
    probs,
    keys,
    values,
    red_n,
    patches,
    sums,
    ff_pack,
    grad,
    ff_full,
    full,
    small,
    wq_l,
    wo_l,
    wk_l,
    wv_l,
    wr_l,
    g_att,
    g_query,
    g_keys,
    g_values,
    g_patch,
    g_scores,
    kb,
    vb,
    tmp,
    acc,
    ff_acc,
    ff_near,
    ff_got,
    big,
    near,
    got,
    small_sum,
    small_got,
    send,
    recv,
):
    blocks = probs.shape[0]
    rows = g_after.shape[0]
    slabs = rows // SLAB
    krows = blocks * KPAD
    first = own_first(blocks)
    part = D // cores
    g1, b1, gr, sr = line(first_gain), line(first_bias), line(reduce_gain), line(reduce_shift)

    wires = Wires(pairs, cores, send, recv)
    core = wires.core
    orders = axis_orders(wires.groups())
    unit = 8 * pairs
    ff_real = ff_pack.shape[0] // cores
    ff_total, total = ff_acc.shape[0], big.shape[1]
    if ff_total > ff_real:
        ff_acc[ff_real:, :] = jnp.zeros((ff_total - ff_real, 128), f32)
        ff_near[ff_real:, :] = jnp.zeros((ff_total - ff_real, 128), f32)
    if total > 20 * part:
        for h in range(cores):
            big[h, 20 * part :, :] = jnp.zeros((total - 20 * part, 128), f32)
    wires.greet()
    ff_chains = []
    for i, (low, high) in enumerate(cut(ff_total, unit, (4 / 26, 10 / 26, 16 / 26, 21 / 26))):
        size = min(high, ff_real) - low
        here = pl.ds(low, size)
        opening = [wires.local(ff_pack.at[rows_of(core * ff_real + low, size)], ff_acc.at[here])]
        if cores > 1:
            opening.append(wires.sibling(ff_pack.at[rows_of(wires.other * ff_real + low, size)], ff_near.at[here]))
        ff_chains.append(
            Chain(
                wires,
                ff_acc,
                ff_near if cores > 1 else None,
                ff_got,
                ff_full,
                low,
                high - low,
                orders[(2, 0, 1, 0, 1)[i]],
                opening,
                [],
            )
        )
    bounds = [2 * part, 12 * part, 17 * part]
    chains = []
    cuts = cut(total, unit, (2 / 25, 8 / 25, 13 / 25, 15 / 25, 18 / 25, 21 / 25, 23 / 25))
    for i, (low, high) in enumerate(cuts):
        here = pl.ds(low, high - low)
        opening, closing = [], []
        if cores > 1:
            opening = [wires.sibling(big.at[wires.other, here], near.at[here])]
            closing = [wires.sibling(full.at[core, here], full.at[core, here])]
        chain = Chain(
            wires,
            big.at[core],
            near if cores > 1 else None,
            got,
            full.at[core],
            low,
            high - low,
            orders[(0, 0, 1, 2, 0, 1, 0, 1)[i]],
            opening,
            closing,
        )
        chain.ready = sum(high > x for x in bounds)
        chains.append(chain)
    plan = Plan()
    plan.add(ff_chains)

    def tick(us, level=None):
        run_steps(plan.after(us))
        if level is not None:
            plan.add([c for c in chains if c.ready == level])
            run_steps(plan.after(0.0))

    def ticks(count, us):
        return [plan.after(us) for _ in range(count)]

    def run_at(index, planned):
        for i, steps in enumerate(planned):
            if steps:
                pl.when(index == i)(partial(run_steps, steps))

    def store(tile, value):
        for t in range(value.shape[1] // 128):
            for h in range(cores):
                big[h, (tile + t) * part : (tile + t + 1) * part, :] = value[
                    h * part : (h + 1) * part, 128 * t : 128 * t + 128
                ]

    tick(0.0)
    wo_l[...] = pack_lane(wo[...])
    wk_l[...] = pack_lane(wkv[:, :D])
    wv_l[...] = pack_lane(wkv[:, D:])
    kb[...] = jnp.zeros_like(kb)
    vb[...] = jnp.zeros_like(vb)
    acc[...] = jnp.zeros_like(acc)
    tick(2.0)
    planned_0 = ticks(slabs, 0.6)

    @pl.loop(0, slabs)
    def _(w):
        g = marks[slab(w), 0:1] * g_after[slab(w), :]
        grad[slab(w), :] = g
        acc[0] += fold(g)
        g_att[slab(w), :] = mm_lane(pack_left(g), wo_l[...])
        run_at(w, planned_0)

    d_wo = mm_rows(attended[...], grad[...])
    store(0, d_wo[:, :256])
    tick(3.5, 0)
    planned_1 = ticks(blocks, 1.8)

    @pl.loop(0, blocks)
    def _(b):
        head_block(values, b, vb)
        here = pl.ds(window(b), WIN)
        first_row = 12 * (b % 2)
        row = lax.broadcasted_iota(jnp.int32, (WIN, D), 0)
        inside = (row >= first_row) & (row < first_row + BLOCK)
        ga = jnp.where(inside, g_att[here, :], 0.0)
        p = probs[b]
        gp = mm_lane(pack_left(ga), head_lane(vb))
        below = head_of_lane(p.shape)
        gs = p * (gp - per_head(below, gp * p, 0.0, jnp.sum)) * (HEAD**-0.5)
        g_scores[b] = gs
        here_k = pl.ds(pl.multiple_of(b * KPAD, 8), KPAD)
        g_values[here_k, :] = head_unblock(tmp, mm_rows(p, ga))
        g_keys[here_k, :] = head_unblock(tmp, mm_rows(gs, query[here, :]))
        run_at(b, planned_1)


    @pl.loop(0, krows // SLAB)
    def _(w):
        gk, gv = g_keys[slab(w), :], g_values[slab(w), :]
        acc[1] += fold(gv)
        g = mm_lane(pack_left(gk), wk_l[...]) + mm_lane(pack_left(gv), wv_l[...])
        n = red_n[slab(w), :D]
        acc[2] += fold(g * n)
        acc[3] += fold(g)
        g = norm_back(g * gr, n, red_n[slab(w), D : D + 1])
        acc[4] += fold(g)
        grad[slab(w), :] = g

    tick(2.0)
    g_red = grad[0:krows, :]
    for pair in range(2):
        d_wr = jnp.concatenate([mm_rows(g_red, patches[2 * pair]), mm_rows(g_red, patches[2 * pair + 1])], 1)
        store(2 + 5 * pair, d_wr)
        tick(2.0, 1 if pair else None)
    reduced = red_n[:, :D] * gr + sr
    d_wk = mm_rows(reduced, g_keys[...])
    d_wv = mm_rows(reduced, g_values[...])
    store(12, jnp.concatenate([d_wk, d_wv], 1))
    tick(2.5, 2)
    for sub in range(4):
        wr_l[sub] = pack_down(wr[:, sub * D : sub * D + D])

    @pl.loop(0, krows // SLAB)
    def _(w):
        packed = pack_left(grad[slab(w), :])
        for sub in range(4):
            g_patch[sub, slab(w), :] = mm(packed, wr_l[sub])

    tick(2.0)
    planned_2 = ticks(blocks, 0.6)

    @pl.loop(0, blocks)
    def _(b):
        head_block(keys, b, kb)
        place_window(g_query, b, mm(triple_left(g_scores[b]), triple_down(head_rows(kb))))
        run_at(b, planned_2)

    wq_l[...] = pack_lane(wq[...])

    @pl.loop(0, slabs)
    def _(w):
        acc[5] += fold(g_query[slab(w), :])
        grad[slab(w), :] = first_n[slab(w), :D] * g1 + b1

    d_wq = mm_rows(grad[...], g_query[...])
    store(17, jnp.concatenate([d_wo[:, 256:], d_wq], 1))
    tick(4.0, 3)
    planned_3 = ticks(slabs, 0.45)

    @pl.loop(0, slabs)
    def _(w):
        g_att[slab(w), :] = mm_lane(pack_left(g_query[slab(w), :]), wq_l[...])
        run_at(w, planned_3)

    planned_4 = ticks(blocks, 0.3)

    @pl.loop(0, blocks)
    def _(b):
        which = kinds[first + b] * 2 + b % 2
        here_k = pl.ds(pl.multiple_of(b * KPAD, 8), KPAD)
        high, low = split(jnp.concatenate([g_patch[sub, here_k, :] for sub in range(4)], 0))
        pick = table[which]
        dims = (((0,), (0,)), ((), ()))
        moved = lax.dot_general(pick, high, dims, preferred_element_type=f32)
        moved = moved + lax.dot_general(pick, low, dims, preferred_element_type=f32)
        g_att[pl.ds(window(b), WIN), :] += moved
        run_at(b, planned_4)

    planned_5 = ticks(slabs, 0.3)

    @pl.loop(0, slabs)
    def _(w):
        n, scale = first_n[slab(w), :D], first_n[slab(w), D : D + 1]
        g = g_att[slab(w), :]
        acc[6] += fold(g * n)
        acc[7] += fold(g)
        grad[slab(w), :] = g_after[slab(w), :] + norm_back(g * g1, n, scale)
        run_at(w, planned_5)

    order = (acc[6], acc[7], acc[5], acc[4], acc[2], acc[3], acc[1], acc[0], sums[0], sums[1], sums[2])
    value = jnp.concatenate([jnp.sum(x, 0, keepdims=True) for x in order] + [jnp.zeros((5, D), f32)], 0)
    value = jnp.concatenate([value, value[:, 256:]], 1)
    for t in range(3):
        small_sum[0, 16 * t : 16 * t + 16, :] = value[:, 128 * t : 128 * t + 128]
    exchange = Exchange(wires, small_sum, small_got)
    plan.add([exchange])
    run_steps(plan.rest())
    for t in range(3):
        small[:, 128 * t : 128 * t + 128] = small_sum[exchange.last, 16 * t : 16 * t + 16, :]


def attention_backward(pairs, cores, kinds, g_after, marks, vecs, wq, wr, wkv, wo, saved, sums, ff_pack):
    rows = g_after.shape[0]
    blocks = rows // BLOCK
    krows = blocks * KPAD
    bits = pairs.bit_length() - 1
    ff_total, total = sum_rows(pairs, cores)
    slots = 15 * (3 + 3 * bits)
    vm = pl.BlockSpec(memory_space=pltpu.VMEM)
    first_n, *saved = saved
    return pl.pallas_call(
        partial(backward_kernel, pairs, cores),
        out_shape=(
            jax.ShapeDtypeStruct((rows, D), f32),
            jax.ShapeDtypeStruct((ff_total, 128), f32),
            jax.ShapeDtypeStruct((cores, total, 128), f32),
            jax.ShapeDtypeStruct((16, 3 * 128), f32),
        ),
        in_specs=[pl.BlockSpec(memory_space=pltpu.SMEM)] + [vm] * 20 + [pl.BlockSpec(memory_space=pl.ANY)],
        out_specs=(vm,) * 4,
        scratch_shapes=[
            pltpu.VMEM((D, 1024), bf16),
            pltpu.VMEM((D, 1024), bf16),
            pltpu.VMEM((D, 1024), bf16),
            pltpu.VMEM((D, 1024), bf16),
            pltpu.VMEM((4, 1024, D), bf16),
            pltpu.VMEM((rows, D), f32),
            pltpu.VMEM((rows, D), f32),
            pltpu.VMEM((krows, D), f32),
            pltpu.VMEM((krows, D), f32),
            pltpu.VMEM((4, krows, D), f32),
            pltpu.VMEM((blocks, WIN, 256), f32),
            pltpu.VMEM((3, 256, 128), f32),
            pltpu.VMEM((3, 256, 128), f32),
            pltpu.VMEM((3, 256, 128), f32),
            pltpu.VMEM((8, 8, D), f32),
            pltpu.VMEM((ff_total, 128), f32),
            pltpu.VMEM((ff_total, 128), f32),
            pltpu.VMEM((ff_total, 128), f32),
            pltpu.VMEM((cores, total, 128), f32),
            pltpu.VMEM((total, 128), f32),
            pltpu.VMEM((total, 128), f32),
            pltpu.VMEM((bits + cores, 48, 128), f32),
            pltpu.VMEM((bits + cores, 48, 128), f32),
            pltpu.SemaphoreType.DMA((slots,)),
            pltpu.SemaphoreType.DMA((slots,)),
        ],
        compiler_params=pltpu.CompilerParams(
            collective_id=0 if pairs * cores > 1 else None, has_side_effects=True, vmem_limit_bytes=63 * MIB
        ),
        name="attention_back",
    )(
        kinds,
        first_n,
        g_after,
        marks,
        jnp.asarray(gather_table(), bf16),
        vecs[0],
        vecs[1],
        vecs[4],
        vecs[5],
        wq,
        wr,
        wkv,
        wo,
        *saved,
        sums,
        ff_pack,
    )


def unpack_kernel(grad, ff, rest, small, grad_t, d_we, d_ws, d_dw, d_be, d_bd, d_wr, d_wkv, d_wq, d_wo, *lines):
    cores = rest.shape[0]
    part = D // cores
    grad_t[...] = grad[...].T
    span = 2 * D + 16
    for t in range(d_we.shape[1] // 128):
        lanes = slice(128 * t, 128 * t + 128)
        d_we[:, lanes] = ff[t * span : t * span + D, :]
        d_ws[:, lanes] = ff[t * span + D : t * span + 2 * D, :]
        d_dw[:, lanes] = ff[t * span + 2 * D : t * span + 2 * D + 9, :]
    for row, ref in ((9, d_be), (10, d_bd)):
        at = 2 * D + row
        parts = [ff[t * span + at : t * span + at + 1, :] for t in range(d_we.shape[1] // 128)]
        ref[...] = jnp.concatenate(parts, 1).reshape(-1)
    for i, ref in enumerate(lines):
        ref[...] = small[i : i + 1, :D].reshape(-1)

    def tile(k):
        return jnp.concatenate([rest[h, k * part : k * part + part, :] for h in range(cores)], 0)

    for t in range(10):
        d_wr[:, 128 * t : 128 * t + 128] = tile(2 + t)
    for t in range(5):
        d_wkv[:, 128 * t : 128 * t + 128] = tile(12 + t)
    mixed = jnp.concatenate([tile(17 + t) for t in range(3)], 1)
    d_wo[...] = jnp.concatenate([tile(0), tile(1), mixed[:, :64]], 1)
    d_wq[...] = mixed[:, 64:]


def unpack(grad, ff, rest, small):
    cores = rest.shape[0]
    rows = grad.shape[0]
    chans = FF // cores
    vm = pl.BlockSpec(memory_space=pltpu.VMEM)
    shapes = [(D, rows), (D, chans), (D, chans), (9, chans), (chans,), (chans,)]
    shapes += [(D, 4 * D), (D, 2 * D), (D, D), (D, D)] + [(D,)] * 11
    return pl.pallas_call(
        unpack_kernel,
        out_shape=tuple(jax.ShapeDtypeStruct(x, f32) for x in shapes),
        in_specs=[vm] * 4,
        out_specs=(vm,) * len(shapes),
        compiler_params=pltpu.CompilerParams(vmem_limit_bytes=60 * MIB),
        name="unpack",
    )(grad, ff, rest, small)


def body(
    pairs,
    cores,
    tokens,
    block_kind,
    first_gain,
    first_bias,
    query_weight,
    query_bias,
    reduce_weight,
    reduce_bias,
    reduce_gain,
    reduce_shift,
    keyval_weight,
    value_bias,
    output_weight,
    output_bias,
    second_gain,
    second_shift,
    expand_weight,
    expand_bias,
    depth_weight,
    depth_bias,
    shrink_weight,
    shrink_bias,
    cotangent,
):
    own_taps = jnp.concatenate(
        [depth_weight, expand_bias[None], depth_bias[None], jnp.zeros((5, expand_bias.shape[0]), f32)], 0
    )
    hidden = [lax.all_gather(x, "hidden", axis=0) for x in (expand_weight, shrink_weight.T, own_taps)]
    vecs = (
        first_gain,
        first_bias,
        query_bias,
        reduce_bias,
        reduce_gain,
        reduce_shift,
        value_bias,
        output_bias,
    )
    late = (second_gain, second_shift, shrink_bias)
    weights = (query_weight, reduce_weight.T, keyval_weight, output_weight)
    after, marks, *saved = attention_forward(block_kind, tokens.T, vecs, *weights)
    result_t, g_after, ff_pack, sums = feed_forward(block_kind, after, cotangent.T, late, hidden)
    grad, ff_sum, rest, small = attention_backward(
        pairs, cores, block_kind, g_after, marks, vecs, *weights, saved, sums, ff_pack.reshape(-1, 128)
    )
    outs = unpack(grad, ff_sum, rest, small)
    grad_t, d_we, d_ws, d_dw, d_be, d_bd, d_wr, d_wkv, d_wq, d_wo, *small = outs
    return (
        result_t.T,
        grad_t.T,
        small[0],
        small[1],
        d_wq,
        small[2],
        d_wr.T,
        small[3],
        small[4],
        small[5],
        d_wkv,
        small[6],
        d_wo,
        small[7],
        small[8],
        small[9],
        d_we,
        d_be,
        d_dw,
        d_bd,
        d_ws.T,
        small[10],
    )


def solution(mesh):
    both = P(("dp", "hidden"), None)
    cols = P(None, "hidden")
    chan = P("hidden")
    deep = P("hidden", None)
    whole = P()
    return jax.shard_map(
        partial(body, mesh.shape["dp"], mesh.shape["hidden"]),
        mesh=mesh,
        in_specs=(both,) + (whole,) * 15 + (cols, chan, cols, chan, deep, whole, both),
        out_specs=(both, both) + (whole,) * 14 + (cols, chan, cols, chan, deep, whole),
        check_vma=False,
    )
```

profile of v0, /device:TPU:0, one launch (start us, length us, event | category | flops | bytes accessed | tf_op | source)
XLA Modules:
  0.0 242.0 jit_solution(9026239443349480174)
XLA Ops:
  7.2 0.0 all-gather.6.cloned.1.call-start
  7.2 0.7 all-gather.6.cloned.1.call-update
  7.9 0.0 all-gather.8.cloned.1.call-start
  8.0 0.7 all-gather.8.cloned.1.call-update
  8.7 0.7 broadcast_in_dim.10
  9.4 0.7 broadcast_in_dim.9
  10.1 0.1 pad.3.clone
  10.1 0.0 copy-start
  10.1 33.7 %attention.1 = (f32[1568,320]{1,0:T(8,128)}, f32[1568,128]{1,0:T(8,128)}, f32[1568,384]{1,0:T(8,128)}, f32[1568,320]{1,0:T(8,128)}, f32[1568,320]{1,0:T(8,128)},...) custom-call(s32[256]{0:T(256)} %kinds.5, ...), custom_call_target="tpu_custom_call" | custom-call | tf_op jit(solution)/shard_map/attention/pallas_call | solution.py:381
  43.8 0.0 copy-done
  43.8 0.1 maximum_maximum_fusion
  43.9 2.6 %all-gather.2 = f32[32,640]{1,0:T(8,128)} all-gather(f32[16,640]{1,0:T(8,128)S(1)} %maximum_maximum_fusion), channel_id=4, replica_groups=mesh['dp'=16,'hidden'=2] {'hidden'}, dimensions={0}, use_global_device_ids=true | all-gather | bytes 122880 | tf_op jit(solution)/shard_map/all_gather | solution.py:1486
  46.5 0.0 all-gather.6.cloned.1.call-done
  46.5 0.0 all-gather.8.cloned.1.call-done
  46.5 77.2 %feed_forward.1 = (f32[320,1568]{1,0:T(8,128)}, f32[1568,320]{1,0:T(8,128)}, f32[10,656,128]{2,1,0:T(8,128)}, f32[3,8,320]{2,1,0:T(8,128)}) custom-call(s32[256]{0:T(256)} %kinds.5, f32[1568,320]{1,0:T(8,128)} %get-tuple-element.61.after, f32[320,1568]{1,0:T(8,128)} %bitcast.16, f32[320]{0:T(512)} %second_gain.1, f32[320]{0:T(512)} %second_shift.1, ...), custom_call_target="tpu_custom_call" | custom-call | tf_op jit(solution)/shard_map/feed_forward/pallas_call | solution.py:810
  123.7 104.2 %attention_back.1 = (f32[1568,320]{1,0:T(8,128)}, f32[3328,128]{1,0:T(8,128)}, f32[2,3200,128]{2,1,0:T(8,128)}, f32[16,384]{1,0:T(8,128)}) custom-call(s32[256]{0:T(256)} %kinds.5, f32[1568,384]{1,0:T(8,128)} %get-tuple-element.63.first_n, f32[1568,320]{1,0:T(8,128)} %get-tuple-element.64.g_after, f32[1568,128]{1,0:T(8,128)} %get-tuple-element.65.marks, ...), custom_call_target="tpu_custom_call" | custom-call | tf_op jit(solution)/shard_map/attention_back/pallas_call | solution.py:1349
  227.9 7.0 %unpack.1 = (f32[320,1568]{1,0:T(8,128)}, f32[320,640]{1,0:T(8,128)}, f32[320,640]{1,0:T(8,128)}, f32[9,640]{1,0:T(8,128)}, f32[640]{0:T(1024)}, /*index=5*/f32[...) custom-call(f32[1568,320]{1,0:T(8,128)} %get-tuple-element.75.grad, ...), custom_call_target="tpu_custom_call" | custom-call | tf_op jit(solution)/shard_map/unpack/pallas_call | solution.py:1446
  (1 shorter events, 0.0 us)
Async XLA Ops:
  7.2 39.3 %all-gather.6.cloned.1.call-start = ((), (), s32[]{:S(2)}) async-start(), calls=%async_computation | async-start | bytes 2457600 | tf_op jit(solution)/shard_map/all_gather | solution.py:1486
  7.9 38.6 %all-gather.8.cloned.1.call-start = ((), (), s32[]{:S(2)}) async-start(), calls=%async_computation.1 | async-start | bytes 2457600 | tf_op jit(solution)/shard_map/all_gather | solution.py:1486
  10.1 33.7 %copy-start = (f32[9,640]{1,0:T(8,128)S(1)}, f32[9,640]{1,0:T(8,128)}, u32[]{:S(2)}) copy-start(f32[9,640]{1,0:T(8,128)} %param.45) | copy-start | bytes 69124
Sparse Core Ops, SparseCore 0:
  9.6 12.6 all-gather.5
  23.8 11.0 all-gather.7
where the time goes:
time: 247 us; the launch traced here: 242 us
  Pallas kernels  222 us (90%)
  between operations  14.4 us (6%)
  blocking collectives  2.61 us (1%)
    pallas_call x1, Pallas kernels, attention_backward(): pl.pallas_call(partial(backward_kernel, pairs, cores), out_shape=(jax.Sha...  104 us
    pallas_call x1, Pallas kernels, feed_forward(): pl.pallas_call(forward_kernel, out_shape=(jax.ShapeDtypeStruct((D, rows),...  77.2 us
    pallas_call x1, Pallas kernels, attention_forward(): pl.pallas_call(attention_kernel, out_shape=(shape(rows, D), shape(rows, 1...  33.7 us
    pallas_call x1, Pallas kernels, unpack(): pl.pallas_call(unpack_kernel, out_shape=tuple((jax.ShapeDtypeStruct(x, f3...  7.03 us
  transfers between devices with their start and end apart: 2, of which 0 were waited for; matrix products, arithmetic and copies ran while one was open for 1% of the time, Pallas kernels for 14%

commit v1 on v0

--- a/solution.py
+++ b/solution.py
@@ -23,6 +23,7 @@
 CHUNK = 256
 CHUNKS = FF // CHUNK
 SLAB = 224
+DEEP = 1024
 PAD = 16
 MIB = 1024 * 1024
 
@@ -284,25 +285,12 @@
     wkv,
     wo,
     after,
-    marks,
-    first_n,
-    query,
-    attended,
-    probs,
-    keys,
-    values,
-    red_n,
-    patches,
-    wq_s,
-    wo_s,
-    wk_s,
-    wv_s,
-    wr_s,
-    tokens,
-    normed,
-    kb,
-    vb,
+    *refs,
 ):
+    held, refs = refs[:9], refs[9:]
+    marks, first_n, query, attended, probs, keys, values, red_n, patches = refs[:9]
+    wq_s, wo_s, wk_s, wv_s, wr_s, tokens, normed, kb, vb, sem = refs[9:]
+    saves = [pltpu.make_async_copy(src, dst, sem.at[i]) for i, (src, dst) in enumerate(zip(refs, held))]
     blocks = probs.shape[0]
     slabs = tokens.shape[0] // SLAB
     first = own_first(blocks)
@@ -326,6 +314,9 @@
         normed[slab(w), :] = n
         query[slab(w), :] = mm(pack_left(n), wq_s[...]) + bq
 
+    saves[1].start()
+    saves[2].start()
+
     @pl.loop(0, blocks)
     def _(b):
         which = kinds[first + b] * 2 + b % 2
@@ -338,6 +329,9 @@
         for sub in range(4):
             patches[sub, rows, :] = got[sub * KPAD : sub * KPAD + KPAD]
 
+    saves[0].start()
+    saves[8].start()
+
     @pl.loop(0, blocks * KPAD // SLAB)
     def _(w):
         acc = br + mm_lane(pack_left(patches[0, slab(w), :]), wr_s[0])
@@ -348,6 +342,9 @@
         packed = pack_left(n * gr + sr)
         keys[slab(w), :] = mm(packed, wk_s[...])
         values[slab(w), :] = mm(packed, wv_s[...]) + bv
+
+    for i in (5, 6, 7):
+        saves[i].start()
 
     @pl.loop(0, blocks)
     def _(b):
@@ -363,10 +360,16 @@
         out = mm(triple_left(p), triple_down(head_rows(vb)))
         place_window(attended, b, out)
 
+    saves[3].start()
+    saves[4].start()
+
     @pl.loop(0, slabs)
     def _(w):
         branch = mm(pack_left(attended[slab(w), :]), wo_s[...]) + bo
         after[slab(w), :] = tokens[slab(w), :] + marks[slab(w), 0:1] * branch
+
+    for save in saves:
+        save.wait()
 
 
 def attention_forward(kinds, tokens_t, vecs, wq, wr, wkv, wo):
@@ -378,23 +381,24 @@
     def shape(*dims):
         return jax.ShapeDtypeStruct(dims, f32)
 
+    saved = (
+        shape(rows, 128),
+        shape(rows, D + 64),
+        shape(rows, D),
+        shape(rows, D),
+        shape(blocks, WIN, 256),
+        shape(krows, D),
+        shape(krows, D),
+        shape(krows, D + 64),
+        shape(4, krows, D),
+    )
     return pl.pallas_call(
         attention_kernel,
-        out_shape=(
-            shape(rows, D),
-            shape(rows, 128),
-            shape(rows, D + 64),
-            shape(rows, D),
-            shape(rows, D),
-            shape(blocks, WIN, 256),
-            shape(krows, D),
-            shape(krows, D),
-            shape(krows, D + 64),
-            shape(4, krows, D),
-        ),
+        out_shape=(shape(rows, D),) + saved,
         in_specs=[pl.BlockSpec(memory_space=pltpu.SMEM)] + [vm] * 16,
-        out_specs=(vm,) * 10,
-        scratch_shapes=[
+        out_specs=(vm,) + (pl.BlockSpec(memory_space=pl.ANY),) * 9,
+        scratch_shapes=[pltpu.VMEM(x.shape, f32) for x in saved]
+        + [
             pltpu.VMEM((1024, D), bf16),
             pltpu.VMEM((1024, D), bf16),
             pltpu.VMEM((1024, D), bf16),
@@ -404,6 +408,7 @@
             pltpu.VMEM((rows, D), f32),
             pltpu.VMEM((3, 256, 128), f32),
             pltpu.VMEM((3, 256, 128), f32),
+            pltpu.SemaphoreType.DMA((9,)),
         ],
         compiler_params=pltpu.CompilerParams(vmem_limit_bytes=60 * MIB),
         name="attention",
@@ -501,10 +506,12 @@
     gx,
     held_act,
     held_gx,
+    dwe,
+    dws,
     sem,
 ):
     rows = after.shape[0]
-    part = rows // 2
+    pieces = rows // SLAB
     per = FF // 128 // own_we.shape[0]
     g2, s2, bs = line(second_gain), line(second_shift), line(shrink_bias)
     first = own_first(8)
@@ -606,7 +613,7 @@
                 taps[c, t, k] = jnp.broadcast_to(pack[2 * c + t, 2 * D + k : 2 * D + k + 1, :], (8, 128))
 
     def own(h):
-        return slice(h * part, (h + 1) * part)
+        return slice(h * SLAB, (h + 1) * SLAB)
 
     def left(ref, h):
         x = ref[own(h), :]
@@ -635,30 +642,47 @@
             jnp.concatenate([x, x[:, :256]], 1), jnp.concatenate([weight[:, :256], weight], 1)
         )
 
-    def weight_task(c, source, turned, row):
-        high, low = source[:, :256], source[:, 256:]
-        value = mm(turned[...], jnp.concatenate([high, high, low], 0))
+    def weight_task(c, source, turned, row, total, k):
+        span = slice(k * DEEP, min((k + 1) * DEEP, 3 * rows))
+        parts = []
+        for i, low in enumerate((0, 0, CHUNK)):
+            start, stop = max(span.start, i * rows) - i * rows, min(span.stop, (i + 1) * rows) - i * rows
+            if start < stop:
+                parts.append(source[start:stop, low : low + CHUNK])
+        value = mm(turned[:, span], jnp.concatenate(parts, 0) if len(parts) > 1 else parts[0])
+        if k > 0:
+            value = value + total[...]
+        if span.stop < 3 * rows:
+            total[...] = value
+            return
         for t in range(2):
             pack[2 * c + t, row : row + D, :] = value[:, 128 * t : 128 * t + 128]
 
     def early_tasks(c, x_outs, g_outs):
-        return [partial(expand_task, c, h, x_outs) for h in range(2)] + [
-            partial(active_grad_task, c, h, g_outs) for h in range(2)
-        ]
+        out = []
+        for h in range(pieces):
+            out += [partial(expand_task, c, h, x_outs), partial(active_grad_task, c, h, g_outs)]
+        return out
 
     def late_tasks(c):
-        return [
-            partial(out_task, c, 0, held_act, ws_l, result),
-            partial(out_task, c, 0, held_gx, we_l, g_second),
-            partial(out_task, c, 1, held_act, ws_l, result),
-            partial(out_task, c, 1, held_gx, we_l, g_second),
-        ]
+        out = []
+        for h in range(pieces):
+            out += [
+                partial(out_task, c, h, held_act, ws_l, result),
+                partial(out_task, c, h, held_gx, we_l, g_second),
+            ]
+        return out
 
     def weight_tasks(c):
-        return [
-            partial(weight_task, c, held_act, branch_t, D),
-            partial(weight_task, c, held_gx, second_t, 0),
-        ]
+        count = -(-3 * rows // DEEP)
+        first_half = [partial(weight_task, c, held_act, branch_t, D, dws, k) for k in range(count)]
+        return first_half, [partial(weight_task, c, held_gx, second_t, 0, dwe, k) for k in range(count)]
+
+    def woven(a, b):
+        out = list(a)
+        for i, task in enumerate(b):
+            out.insert(round((i + 1) * len(a) / (len(b) + 1)) + i, task)
+        return out
 
     def at(r):
         return slice(8 * r, 8 * r + 8)
@@ -765,15 +789,15 @@
     @pl.loop(0, CHUNKS)
     def _(c):
         before = jnp.maximum(c - 1, 0)
-        item(c, 0, xs0, ga0, late_tasks(before) + weight_tasks(before)[:1])
+        item(c, 0, xs0, ga0, woven(late_tasks(before), weight_tasks(before)[0]))
         later = jnp.minimum(c + 1, CHUNKS - 1)
-        item(c, 1, xs1, ga1, early_tasks(later, (xs0, nx1), (ga0, ng1)) + weight_tasks(before)[1:])
+        item(c, 1, xs1, ga1, woven(early_tasks(later, (xs0, nx1), (ga0, ng1)), weight_tasks(before)[1]))
         xs1[...] = nx1[...]
         ga1[...] = ng1[...]
         held_act[...] = act[...]
         held_gx[...] = gx[...]
 
-    for task in late_tasks(CHUNKS - 1) + weight_tasks(CHUNKS - 1):
+    for task in late_tasks(CHUNKS - 1) + sum(weight_tasks(CHUNKS - 1), []):
         task()
     for c in range(CHUNKS):
         for t in range(2):
@@ -834,6 +858,7 @@
         ]
         + [tile] * 9
         + [half] * 4
+        + [pltpu.VMEM((D, CHUNK), f32)] * 2
         + [pltpu.SemaphoreType.DMA((6 * CHUNKS,))],
         compiler_params=pltpu.CompilerParams(vmem_limit_bytes=63 * MIB),
         name="feed_forward",
@@ -1060,7 +1085,7 @@
     pairs,
     cores,
     kinds,
-    first_n,
+    first_n_from,
     g_after,
     marks,
     table,
@@ -1072,6 +1097,20 @@
     wr,
     wkv,
     wo,
+    query_from,
+    attended_from,
+    probs_from,
+    keys_from,
+    values_from,
+    red_n_from,
+    patches_from,
+    sums,
+    ff_pack,
+    grad,
+    ff_full,
+    full,
+    small,
+    first_n,
     query,
     attended,
     probs,
@@ -1079,12 +1118,6 @@
     values,
     red_n,
     patches,
-    sums,
-    ff_pack,
-    grad,
-    ff_full,
-    full,
-    small,
     wq_l,
     wo_l,
     wk_l,
@@ -1176,6 +1209,19 @@
         )
         chain.ready = sum(high > x for x in bounds)
         chains.append(chain)
+    fetch = {
+        name: wires.local(src, dst)
+        for name, src, dst in (
+            ("attended", attended_from, attended),
+            ("values", values_from, values),
+            ("probs", probs_from, probs),
+            ("query", query_from, query),
+            ("red_n", red_n_from, red_n),
+            ("patches", patches_from, patches),
+            ("keys", keys_from, keys),
+            ("first_n", first_n_from, first_n),
+        )
+    }
     plan = Plan()
     plan.add(ff_chains)
 
@@ -1201,6 +1247,8 @@
                 ]
 
     tick(0.0)
+    for c in fetch.values():
+        c.start()
     wo_l[...] = pack_lane(wo[...])
     wk_l[...] = pack_lane(wkv[:, :D])
     wv_l[...] = pack_lane(wkv[:, D:])
@@ -1218,10 +1266,13 @@
         g_att[slab(w), :] = mm_lane(pack_left(g), wo_l[...])
         run_at(w, planned_0)
 
+    fetch["attended"].wait()
     d_wo = mm_rows(attended[...], grad[...])
     store(0, d_wo[:, :256])
     tick(3.5, 0)
     planned_1 = ticks(blocks, 1.8)
+    for name in ("values", "probs", "query"):
+        fetch[name].wait()
 
     @pl.loop(0, blocks)
     def _(b):
@@ -1241,6 +1292,9 @@
         g_keys[here_k, :] = head_unblock(tmp, mm_rows(gs, query[here, :]))
         run_at(b, planned_1)
 
+    fetch["red_n"].wait()
+    fetch["patches"].wait()
+
 
     @pl.loop(0, krows // SLAB)
     def _(w):
@@ -1276,6 +1330,8 @@
 
     tick(2.0)
     planned_2 = ticks(blocks, 0.6)
+    fetch["keys"].wait()
+    fetch["first_n"].wait()
 
     @pl.loop(0, blocks)
     def _(b):
@@ -1344,7 +1400,7 @@
     bits = pairs.bit_length() - 1
     ff_total, total = sum_rows(pairs, cores)
     slots = 15 * (3 + 3 * bits)
-    vm = pl.BlockSpec(memory_space=pltpu.VMEM)
+    vm, far = pl.BlockSpec(memory_space=pltpu.VMEM), pl.BlockSpec(memory_space=pl.ANY)
     first_n, *saved = saved
     return pl.pallas_call(
         partial(backward_kernel, pairs, cores),
@@ -1354,9 +1410,10 @@
             jax.ShapeDtypeStruct((cores, total, 128), f32),
             jax.ShapeDtypeStruct((16, 3 * 128), f32),
         ),
-        in_specs=[pl.BlockSpec(memory_space=pltpu.SMEM)] + [vm] * 20 + [pl.BlockSpec(memory_space=pl.ANY)],
+        in_specs=[pl.BlockSpec(memory_space=pltpu.SMEM), far] + [vm] * 11 + [far] * 7 + [vm, far],
         out_specs=(vm,) * 4,
-        scratch_shapes=[
+        scratch_shapes=[pltpu.VMEM(x.shape, f32) for x in (first_n, *saved)]
+        + [
             pltpu.VMEM((D, 1024), bf16),
             pltpu.VMEM((D, 1024), bf16),
             pltpu.VMEM((D, 1024), bf16),

time: 247 us -> 237 us (0.960)
  Pallas kernels: 222 us -> 213 us
    pallas_call x1, Pallas kernels: 33.7 us -> 29.7 us  [attention_forward(): pl.pallas_call(attention_kernel, out_shape=(shape(rows, D),) + saved, in_...]
    pallas_call x1, Pallas kernels: 104 us -> 100 us  [attention_backward(): pl.pallas_call(partial(backward_kernel, pairs, cores), out_shape=(jax.Sha...]
  transfers between devices with their start and end apart: 2 -> 2, of which waited for: 0 -> 0; matrix products, arithmetic and copies ran while one was open for 1% -> 1% of each run, Pallas kernels for 14% -> 13%
where the time goes in v1:
time: 237 us; the launch traced here: 233 us
  Pallas kernels  213 us (90%)
  between operations  14.6 us (6%)
  blocking collectives  2.61 us (1%)
    pallas_call x1, Pallas kernels, attention_backward(): pl.pallas_call(partial(backward_kernel, pairs, cores), out_shape=(jax.Sha...  100 us
    pallas_call x1, Pallas kernels, feed_forward(): pl.pallas_call(forward_kernel, out_shape=(jax.ShapeDtypeStruct((D, rows),...  75.4 us
    pallas_call x1, Pallas kernels, attention_forward(): pl.pallas_call(attention_kernel, out_shape=(shape(rows, D),) + saved, in_...  29.7 us
    pallas_call x1, Pallas kernels, unpack(): pl.pallas_call(unpack_kernel, out_shape=tuple((jax.ShapeDtypeStruct(x, f3...  7.03 us
  transfers between devices with their start and end apart: 2, of which 0 were waited for; matrix products, arithmetic and copies ran while one was open for 1% of the time, Pallas kernels for 13%

profile of v1, /device:TPU:0, one launch (start us, length us, event | category | flops | bytes accessed | tf_op | source)
XLA Modules:
  0.0 232.7 jit_solution(4203130329244430361)
XLA Ops:
  7.2 0.0 all-gather.6.cloned.1.call-start
  7.2 0.7 all-gather.6.cloned.1.call-update
  7.9 0.0 all-gather.8.cloned.1.call-start
  8.0 0.7 all-gather.8.cloned.1.call-update
  8.7 0.7 broadcast_in_dim.10
  9.4 0.7 broadcast_in_dim.9
  10.1 0.1 pad.3.clone
  10.1 0.0 copy-start
  10.1 29.7 %attention.1 = (f32[1568,320]{1,0:T(8,128)}, f32[1568,128]{1,0:T(8,128)}, f32[1568,384]{1,0:T(8,128)}, f32[1568,320]{1,0:T(8,128)}, f32[1568,320]{1,0:T(8,128)},...) custom-call(s32[256]{0:T(256)} %kinds.5, ...), custom_call_target="tpu_custom_call" | custom-call | tf_op jit(solution)/shard_map/attention/pallas_call | solution.py:395
  39.9 0.0 copy-done
  39.9 0.1 maximum_maximum_fusion
  40.0 2.6 %all-gather.2 = f32[32,640]{1,0:T(8,128)} all-gather(f32[16,640]{1,0:T(8,128)S(1)} %maximum_maximum_fusion), channel_id=4, replica_groups=mesh['dp'=16,'hidden'=2] {'hidden'}, dimensions={0}, use_global_device_ids=true | all-gather | bytes 122880 | tf_op jit(solution)/shard_map/all_gather | solution.py:1543
  42.6 0.0 all-gather.6.cloned.1.call-done
  42.6 0.0 all-gather.8.cloned.1.call-done
  42.6 75.4 %feed_forward.1 = (f32[320,1568]{1,0:T(8,128)}, f32[1568,320]{1,0:T(8,128)}, f32[10,656,128]{2,1,0:T(8,128)}, f32[3,8,320]{2,1,0:T(8,128)}) custom-call(s32[256]{0:T(256)} %kinds.5, f32[1568,320]{1,0:T(8,128)} %get-tuple-element.61.after, f32[320,1568]{1,0:T(8,128)} %bitcast.16, f32[320]{0:T(512)} %second_gain.1, f32[320]{0:T(512)} %second_shift.1, ...), custom_call_target="tpu_custom_call" | custom-call | tf_op jit(solution)/shard_map/feed_forward/pallas_call | solution.py:834
  118.0 100.4 %attention_back.1 = (f32[1568,320]{1,0:T(8,128)}, f32[3328,128]{1,0:T(8,128)}, f32[2,3200,128]{2,1,0:T(8,128)}, f32[16,384]{1,0:T(8,128)}) custom-call(s32[256]{0:T(256)} %kinds.5, f32[1568,384]{1,0:T(8,128)} %get-tuple-element.63.first_n_from, f32[1568,320]{1,0:T(8,128)} %get-tuple-element.64.g_after, f32[1568,128]{1,0:T(8,128)} %get-tuple-element.65.marks, ...), custom_call_target="tpu_custom_call" | custom-call | tf_op jit(solution)/shard_map/attention_back/pallas_call | solution.py:1405
  218.4 7.0 %unpack.1 = (f32[320,1568]{1,0:T(8,128)}, f32[320,640]{1,0:T(8,128)}, f32[320,640]{1,0:T(8,128)}, f32[9,640]{1,0:T(8,128)}, f32[640]{0:T(1024)}, /*index=5*/f32[...) custom-call(f32[1568,320]{1,0:T(8,128)} %get-tuple-element.75.grad, ...), custom_call_target="tpu_custom_call" | custom-call | tf_op jit(solution)/shard_map/unpack/pallas_call | solution.py:1503
  (1 shorter events, 0.0 us)
Async XLA Ops:
  7.2 35.4 %all-gather.6.cloned.1.call-start = ((), (), s32[]{:S(2)}) async-start(), calls=%async_computation | async-start | bytes 2457600 | tf_op jit(solution)/shard_map/all_gather | solution.py:1543
  7.9 34.6 %all-gather.8.cloned.1.call-start = ((), (), s32[]{:S(2)}) async-start(), calls=%async_computation.1 | async-start | bytes 2457600 | tf_op jit(solution)/shard_map/all_gather | solution.py:1543
  10.1 29.7 %copy-start = (f32[9,640]{1,0:T(8,128)S(1)}, f32[9,640]{1,0:T(8,128)}, u32[]{:S(2)}) copy-start(f32[9,640]{1,0:T(8,128)} %param.45) | copy-start | bytes 69124
Sparse Core Ops, SparseCore 0:
  9.6 12.6 all-gather.5
  23.8 11.1 all-gather.7
